TPU v7x, 128 devices: a whole 4x4x4 slice. The times are simulated.
128 devices in a mesh: tile: 16 (over z, y), seq: 8 (over x, core).
Axes of the slice: x: 4, y: 4, z: 4, core: 2. Of those that a mesh axis runs over, the one named last changes fastest.
Arguments:
- cls_tokens: bfloat16 [16384, 1536], P(('tile', 'seq')), may hold values from -6 to 6
- norm_gain: float32 [1536], replicated, may hold values from 0.5 to 1.5
- w_gate: bfloat16 [1536, 4096], P(None, 'tile'), may hold values from -0.15625 to 0.15625
- w_up: bfloat16 [1536, 4096], P(None, 'tile'), may hold values from -0.15625 to 0.15625
- w_down: bfloat16 [4096, 1536], P('tile'), may hold values from -0.09375 to 0.09375
- layer_scale: float32 [1536], replicated, may hold values from 0.25 to 1.75
- final_gain: float32 [1536], replicated, may hold values from 0.5 to 1.5
- w_embed: bfloat16 [1536, 768], replicated, may hold values from -0.15625 to 0.15625
- dest_pos: int32 [16384], P(('tile', 'seq')), may hold values from 0 to 16383, as said below
- tile_coords: int32 [2, 16384], P(None, ('tile', 'seq')), may hold values from 0 to 999
- attn_gain: float32 [768], replicated, may hold values from 0.5 to 1.5
- w_qkv: bfloat16 [768, 2304], replicated, may hold values from -4 to 4
- offsets: int32 [12], replicated, may hold values from 0 to 15
- w_out: bfloat16 [768, 768], replicated, may hold values from -0.21875 to 0.21875
Outputs:
- slide_out: bfloat16 [16384, 768], P(('tile', 'seq'))
Inputs may be any that keep to these rules, and one draw needn't show every extreme that they name: dest_pos holds each number of 0 to 16383 once; the 128 rows of one device go to the devices of the slide order in groups of 0, 1 or 2 rows a device, some pair carrying 2; every device receives 128 rows, 2 of them from the device 128 / 2 places before it in the slide order, counted round.
All inputs are finite; a program needn't handle non-finite values.
Results may differ from a plain program's by a relative error of at most 0.018.
Values may be sent and summed in bfloat16 or wider, within the bound.
No kernel may reach another device: no remote copies, remote signals or barrier semaphores. Data moves between devices by JAX's collectives and lax.ppermute only.
A program may use at most 128 MiB of HBM per device.

v0:
```python
import jax
import jax.numpy as jnp
from jax import lax
from jax.sharding import PartitionSpec as P

HEAD_COUNT = 12
HEAD_WIDTH = 64
SEGMENT_SPACING = 16


def layer_norm(sender_rows, gain):
    average = jnp.mean(sender_rows, axis=-1, keepdims=True)
    centered = sender_rows - average
    variance = jnp.mean(centered * centered, axis=-1, keepdims=True)
    return centered * lax.rsqrt(variance + 1e-06) * gain


def position_table(coords, hidden_width):
    quarter = hidden_width // 4
    frequency = 1.0 / 10000.0 ** (jnp.arange(quarter).astype(jnp.float32) / quarter)
    along_x = coords[:, 0:1].astype(jnp.float32) * frequency[None, :]
    along_y = coords[:, 1:2].astype(jnp.float32) * frequency[None, :]
    return jnp.concatenate(
        [jnp.sin(along_x), jnp.cos(along_x), jnp.sin(along_y), jnp.cos(along_y)], axis=1
    )


def attend(queries, key_rows, values):
    score_scale = queries.shape[-1] ** (-0.5)
    scores = (
        jnp.einsum("qhd,khd->hqk", queries, key_rows, preferred_element_type=jnp.float32)
        * score_scale
    )
    highest = jnp.max(scores, axis=-1, keepdims=True)
    weights = jnp.exp(scores - highest)
    totals = jnp.sum(weights, axis=-1, keepdims=True)
    mixed_rows = jnp.einsum(
        "hqk,khd->qhd", weights.astype(jnp.bfloat16), values, preferred_element_type=jnp.float32
    )
    result = mixed_rows / jnp.transpose(totals, (1, 0, 2))
    logsum = jnp.transpose((highest + jnp.log(totals))[:, :, 0])
    return (result, logsum)


def body(
    cls_tokens,
    norm_gain,
    w_gate,
    w_up,
    w_down,
    layer_scale,
    final_gain,
    w_embed,
    dest_pos,
    tile_coords,
    attn_gain,
    w_qkv,
    offsets,
    w_out,
):
    resident_rows = cls_tokens.shape[0]
    tokens = cls_tokens.astype(jnp.float32)
    normed = layer_norm(tokens, norm_gain).astype(jnp.bfloat16)
    shard_rows = lax.all_gather(normed, "tile", axis=0, tiled=True)
    gate_proj = jnp.dot(shard_rows, w_gate, preferred_element_type=jnp.float32)
    upward = jnp.dot(shard_rows, w_up, preferred_element_type=jnp.float32)
    hidden = (jax.nn.silu(gate_proj) * upward).astype(jnp.bfloat16)
    projected = lax.psum_scatter(
        jnp.dot(hidden, w_down, preferred_element_type=jnp.float32),
        "tile",
        scatter_dimension=0,
        tiled=True,
    )
    mixed_rows = tokens + layer_scale * projected
    final_rows = layer_norm(mixed_rows, final_gain).astype(jnp.bfloat16)
    embedded = jnp.dot(final_rows, w_embed, preferred_element_type=jnp.float32).astype(jnp.bfloat16)
    hidden_width = embedded.shape[1]
    tile_count = lax.axis_size("tile")
    seq_count = lax.axis_size("seq")
    devices = tile_count * seq_count
    capacity = 2 * max(1, resident_rows // devices)
    target = dest_pos // resident_rows
    row_ids = jnp.arange(resident_rows)
    earlier = (target[:, None] == target[None, :]) & (row_ids[None, :] < row_ids[:, None])
    slot_index = jnp.sum(earlier.astype(jnp.int32), axis=1)
    where_to = target * capacity + slot_index
    payload = jnp.zeros((devices * capacity, hidden_width), jnp.bfloat16).at[where_to].set(embedded)
    meta_rows = jnp.stack([dest_pos, tile_coords[0], tile_coords[1]], axis=1)
    meta_table = jnp.full((devices * capacity, 3), -1, jnp.int32).at[where_to].set(meta_rows)
    received, received_meta = (
        lax.all_to_all(
            payload.reshape(devices, capacity, hidden_width),
            ("tile", "seq"),
            split_axis=0,
            concat_axis=0,
            tiled=True,
        ),
        lax.all_to_all(
            meta_table.reshape(devices, capacity, 3),
            ("tile", "seq"),
            split_axis=0,
            concat_axis=0,
            tiled=True,
        ),
    )
    flat_rows = received.reshape(-1, hidden_width)
    flat_meta = received_meta.reshape(-1, 3)
    is_live = flat_meta[:, 0] >= 0
    local_slot = jnp.where(is_live, flat_meta[:, 0] % resident_rows, resident_rows)
    placed = (
        jnp.zeros((resident_rows, hidden_width), jnp.bfloat16)
        .at[local_slot]
        .set(flat_rows, mode="drop")
    )
    coords = (
        jnp.zeros((resident_rows, 2), jnp.int32).at[local_slot].set(flat_meta[:, 1:], mode="drop")
    )
    seq_in = placed.astype(jnp.float32) + position_table(coords, hidden_width)
    normed_seq = layer_norm(seq_in, attn_gain).astype(jnp.bfloat16)
    qkv = jnp.dot(normed_seq, w_qkv, preferred_element_type=jnp.float32).astype(jnp.bfloat16)
    queries = qkv[:, :hidden_width]
    keys_values = qkv[:, hidden_width:]
    segment_kv = lax.all_gather(keys_values, "seq", axis=0, tiled=True)
    near_out, nearby_logsumexp = attend(
        queries.reshape(resident_rows, HEAD_COUNT, HEAD_WIDTH),
        segment_kv[:, :hidden_width].reshape(-1, HEAD_COUNT, HEAD_WIDTH),
        segment_kv[:, hidden_width:].reshape(-1, HEAD_COUNT, HEAD_WIDTH),
    )
    kept_rows = jnp.arange(SEGMENT_SPACING, dtype=jnp.int32)[:, None] == offsets[None, :]

    def select(sender_rows, stacked_rows):
        head_grouped = sender_rows.reshape(
            resident_rows // SEGMENT_SPACING, SEGMENT_SPACING, stacked_rows, HEAD_COUNT, HEAD_WIDTH
        )
        sampled_rows = jnp.sum(
            jnp.where(
                kept_rows[None, :, None, :, None], head_grouped, jnp.zeros((), sender_rows.dtype)
            ),
            axis=1,
        )
        return sampled_rows.reshape(resident_rows // SEGMENT_SPACING, stacked_rows * hidden_width)

    far_kv = lax.all_gather(select(keys_values, 2), ("tile", "seq"), axis=0, tiled=True)
    far_out, far_lse = attend(
        select(queries, 1).reshape(-1, HEAD_COUNT, HEAD_WIDTH),
        far_kv[:, :hidden_width].reshape(-1, HEAD_COUNT, HEAD_WIDTH),
        far_kv[:, hidden_width:].reshape(-1, HEAD_COUNT, HEAD_WIDTH),
    )
    far_full = jnp.where(kept_rows[None, :, :, None], far_out[:, None], 0.0).reshape(
        resident_rows, HEAD_COUNT, HEAD_WIDTH
    )
    nearby_grouped = nearby_logsumexp.reshape(
        resident_rows // SEGMENT_SPACING, SEGMENT_SPACING, HEAD_COUNT
    )
    far_share = jnp.where(
        kept_rows[None], 1.0 / (1.0 + jnp.exp(nearby_grouped - far_lse[:, None])), 0.0
    ).reshape(resident_rows, HEAD_COUNT)
    combined = (1.0 - far_share)[:, :, None] * near_out + far_share[:, :, None] * far_full
    attn_rows = combined.reshape(resident_rows, hidden_width).astype(jnp.bfloat16)
    return (seq_in + jnp.dot(attn_rows, w_out, preferred_element_type=jnp.float32)).astype(
        jnp.bfloat16
    )


def solution(mesh):
    in_specs = (
        P(("tile", "seq"), None),
        P(),
        P(None, "tile"),
        P(None, "tile"),
        P("tile", None),
        P(),
        P(),
        P(),
        P(("tile", "seq")),
        P(None, ("tile", "seq")),
        P(),
        P(),
        P(),
        P(),
    )
    out_specs = P(("tile", "seq"), None)
    return jax.shard_map(body, mesh=mesh, in_specs=in_specs, out_specs=out_specs, check_vma=False)
```

profile of v0, /device:TPU:1, one launch (start us, length us, event | category | flops | bytes accessed | tf_op | source)
XLA Modules:
  0.0 357.2 jit_solution(11485548192163310712)
XLA Ops:
  9.1 2.0 fusion.33
  11.2 64.7 %all-gather.4.cloned.1.call-done = bf16[2048,1536]{1,0:T(8,128)(2,1)} async-done(((bf16[128,1536]{1,0:T(8,128)(2,1)}), bf16[2048,1536]{1,0:T(8,128)(2,1)}) %all-gather.4.cloned.1.call-update) | async-done | bytes 6291472 | tf_op jit(solution)/shard_map/all_gather | solution.py:64
  75.9 6.1 %fusion.70 = f32[2048,256]{1,0:T(8,128)} fusion(bf16[2048,1536]{1,0:T(8,128)(2,1)} %all-gather.4.cloned.1.call-done, bf16[1536,256]{1,0:T(8,128)(2,1)} %param.16), kind=kOutput, calls=%fused_computation.112 | convolution fusion | flops 1610612736 | bytes 9175040 | tf_op jit(solution)/shard_map/dot_general | solution.py:65
  82.0 14.6 %fusion.7 = f32[2048,1536]{1,0:T(8,128)} fusion(bf16[256,1536]{1,0:T(8,128)(2,1)} %param.18, bf16[2048,1536]{1,0:T(8,128)(2,1)} %all-gather.4.cloned.1.call-done, bf16[1536,256]{1,0:T(8,128)(2,1)} %param.17, f32[2048,256]{1,0:T(8,128)} %fusion.70), kind=kOutput, calls=%fused_computation.14 | convolution fusion | flops 3224371200 | bytes 22544384 | tf_op jit(solution)/shard_map/dot_general | solution.py:69
  103.8 8.3 %all-to-all-start = ((s32[128,2,3]{2,1,0:T(2,128)}), s32[128,2,3]{2,1,0:T(2,128)}, u32[]{:S(2)}, u32[]{:S(2)}) async-start(s32[128,2,3]{2,1,0:T(2,128)} %bitcast.76), calls=%async_computation | async-start | bytes 262144 | tf_op jit(solution)/shard_map/all_to_all | solution.py:98
  112.8 9.2 %all-to-all-done = s32[128,2,3]{2,1,0:T(2,128)} async-done(((s32[128,2,3]{2,1,0:T(2,128)}), s32[128,2,3]{2,1,0:T(2,128)}, u32[]{:S(2)}, u32[]{:S(2)}) %all-to-all-start) | async-done | bytes 3104 | tf_op jit(solution)/shard_map/all_to_all | solution.py:98
  123.5 68.9 %reduce-scatter.2.cloned.1.call-done = f32[128,1536]{1,0:T(8,128)} async-done(((f32[2048,1536]{1,0:T(8,128)}), f32[128,1536]{1,0:T(8,128)}) %reduce-scatter.2.cloned.1.call-update) | async-done | bytes 786448 | tf_op jit(solution)/shard_map/reduce_scatter | solution.py:68
  195.4 2.9 convolution_convert_fusion.1
  198.3 2.3 scatter_custom_fusion.1
  200.6 1.9 reshape.194
  202.5 7.8 %all-to-all-start.1 = ((bf16[128,2,768]{2,1,0:T(2,128)(2,1)}), bf16[128,2,768]{2,1,0:T(2,128)(2,1)}, u32[]{:S(2)}, u32[]{:S(2)}) async-start(bf16[128,2,768]{2,1,0:T(2,128)(2,1)} %reshape.194), calls=%async_computation.2 | async-start | bytes 786432 | tf_op jit(solution)/shard_map/all_to_all | solution.py:91
  211.0 2.2 scatter_custom_fusion.3
  214.3 2.5 multiply_sine_fusion.1
  216.7 5.6 %all-to-all-done.1 = bf16[128,2,768]{2,1,0:T(2,128)(2,1)} async-done(((bf16[128,2,768]{2,1,0:T(2,128)(2,1)}), bf16[128,2,768]{2,1,0:T(2,128)(2,1)}, u32[]{:S(2)}, u32[]{:S(2)}) %all-to-all-start.1) | async-done | bytes 393248 | tf_op jit(solution)/shard_map/all_to_all | solution.py:91
  222.3 1.9 reshape.224
  224.2 2.7 scatter_custom_fusion.2
  231.0 2.6 reshape.199
  233.5 2.2 select_reduce_fusion
  242.8 2.1 reshape.198
  246.8 8.7 %all-gather.6.cloned.1.call-done = bf16[1024,1536]{1,0:T(8,128)(2,1)} async-done(((bf16[128,1536]{1,0:T(8,128)(2,1)}), bf16[1024,1536]{1,0:T(8,128)(2,1)}) %all-gather.6.cloned.1.call-update) | async-done | bytes 3145744 | tf_op jit(solution)/shard_map/all_gather | solution.py:123
  255.4 3.8 %fusion.68 = (bf16[1024,768]{1,0:T(8,128)(2,1)}, bf16[1024,768]{1,0:T(8,128)(2,1)}) fusion(bf16[1024,1536]{1,0:T(8,128)(2,1)} %all-gather.6.cloned.1.call-done), kind=kLoop, calls=%fused_computation.110 | loop fusion | bytes 6291456 | tf_op jit(solution)/shard_map/slice | solution.py:126
  259.2 2.6 copy.82
  261.9 2.6 copy.85
  264.5 2.6 multiply_reduce_fusion
  267.1 2.7 copy-done.1
  271.7 52.7 %all-gather.8.cloned.1.call-done = bf16[1024,1536]{1,0:T(8,128)(2,1)} async-done(((bf16[8,1536]{1,0:T(8,128)(2,1)}), bf16[1024,1536]{1,0:T(8,128)(2,1)}) %all-gather.8.cloned.1.call-update) | async-done | bytes 3145744 | tf_op jit(solution)/shard_map/all_gather | solution.py:143
  324.3 3.8 %fusion.67 = (bf16[1024,768]{1,0:T(8,128)(2,1)}, bf16[1024,768]{1,0:T(8,128)(2,1)}) fusion(bf16[1024,1536]{1,0:T(8,128)(2,1)} %all-gather.8.cloned.1.call-done), kind=kLoop, calls=%fused_computation.109 | loop fusion | bytes 6291456 | tf_op jit(solution)/shard_map/slice | solution.py:146
  328.1 2.6 copy.83
  336.2 2.6 copy.86
  338.8 2.1 fusion.15
  341.9 2.1 copy.89
  344.8 4.8 %fusion.26 = bf16[128,12,64]{0,2,1:T(8,128)(2,1)S(1)} fusion(bf16[1024,12,64]{0,2,1:T(8,128)(2,1)} %bitcast.74, f32[12,128,1024]{2,1,0:T(8,128)} %copy-done.1, f32[12,128]{1,0:T(8,128)S(1)} %get-tuple-element.23, f32[128,12,64]{0,2,1:T(8,128)} %copy.89, f32[128,12]{0,1:T(8,128)S(1)} %get-tuple-element.8, f32[128,12]{0,1:T(8,128)} %bitcast.79, ...), kind=kOutput, calls=%fused_computation.33 | convolution fusion | flops 206635008 | bytes 8480256 | tf_op jit(solution)/shard_map/hqk,khd->qhd/dot_general | solution.py:37
  (77 shorter events, 39.8 us)
Async XLA Ops:
  6.5 222.0 %copy-start = (bf16[768,2304]{1,0:T(8,128)(2,1)S(1)}, bf16[768,2304]{1,0:T(8,128)(2,1)}, u32[]{:S(2)}) copy-start(bf16[768,2304]{1,0:T(8,128)(2,1)} %param.25) | copy-start | bytes 10616836
  6.5 69.4 %all-gather.4.cloned.1.call-start = ((), (), s32[]{:S(2)}) async-start(), calls=%async_computation.3 | async-start | bytes 6684672 | tf_op jit(solution)/shard_map/all_gather | solution.py:64
  11.1 181.2 %reduce-scatter.2.cloned.1.call-start = ((), (), s32[]{:S(2)}) async-start(), calls=%async_computation.4 | async-start | bytes 13369344 | tf_op jit(solution)/shard_map/reduce_scatter | solution.py:68
  96.6 95.8 %copy-start.9 = (f32[1536]{0:T(1024)S(1)}, f32[1536]{0:T(1024)}, u32[]{:S(2)}) copy-start(f32[1536]{0:T(1024)} %param.19) | copy-start | bytes 18436
  96.6 98.8 %copy-start.11 = (f32[1536]{0:T(1024)S(1)}, f32[1536]{0:T(1024)}, u32[]{:S(2)}) copy-start(f32[1536]{0:T(1024)} %param.20) | copy-start | bytes 18436
  103.8 18.1 %all-to-all-start = ((s32[128,2,3]{2,1,0:T(2,128)}), s32[128,2,3]{2,1,0:T(2,128)}, u32[]{:S(2)}, u32[]{:S(2)}) async-start(s32[128,2,3]{2,1,0:T(2,128)} %bitcast.76), calls=%async_computation | async-start | bytes 262144 | tf_op jit(solution)/shard_map/all_to_all | solution.py:98
  192.4 3.0 copy-start.2
  192.4 3.0 copy-start.3
  200.6 28.0 %copy-start.12 = (f32[768]{0:T(1024)S(1)}, f32[768]{0:T(1024)}, u32[]{:S(2)}) copy-start(f32[768]{0:T(1024)} %param.24) | copy-start | bytes 9220
  202.5 19.8 %all-to-all-start.1 = ((bf16[128,2,768]{2,1,0:T(2,128)(2,1)}), bf16[128,2,768]{2,1,0:T(2,128)(2,1)}, u32[]{:S(2)}, u32[]{:S(2)}) async-start(bf16[128,2,768]{2,1,0:T(2,128)(2,1)} %reshape.194), calls=%async_computation.2 | async-start | bytes 786432 | tf_op jit(solution)/shard_map/all_to_all | solution.py:91
  210.3 45.2 %all-gather.6.cloned.1.call-start = ((), (), s32[]{:S(2)}) async-start(), calls=%async_computation.5 | async-start | bytes 3538944 | tf_op jit(solution)/shard_map/all_gather | solution.py:123
  228.3 0.9 copy-start.4
  228.5 2.4 copy-start.13
  229.2 0.8 copy-start.7
  230.9 93.4 %all-gather.8.cloned.1.call-start = ((), (), s32[]{:S(2)}) async-start(), calls=%async_computation.6 | async-start | bytes 3170304 | tf_op jit(solution)/shard_map/all_gather | solution.py:143
  267.1 2.7 copy-start.1
  332.5 0.7 copy-start.6
  333.5 0.6 copy-start.10
  344.8 4.8 %copy-start.5 = (f32[128,768]{1,0:T(8,128)S(1)}, f32[128,768]{1,0:T(8,128)}, u32[]{:S(2)}) copy-start(f32[128,768]{1,0:T(8,128)} %copy-done.4) | copy-start | bytes 1179652
  344.8 4.8 %copy-start.8 = (bf16[768,768]{1,0:T(8,128)(2,1)S(1)}, bf16[768,768]{1,0:T(8,128)(2,1)}, u32[]{:S(2)}) copy-start(bf16[768,768]{1,0:T(8,128)(2,1)} %param.27) | copy-start | bytes 3538948
Sparse Core Ops, SparseCore 0:
  11.3 64.6 all-gather.3
  96.7 95.5 reduce-scatter.1
  231.0 24.3 all-gather.5
  258.4 65.8 all-gather.7
where the time goes:
time: 358 us; the launch traced here: 357 us
  waiting for transfers between devices  210 us (59%)
  local copies, waits for them, and re-layouts  56.9 us (16%)
  matrix products  36.7 us (10%)
  other arithmetic  24.2 us (7%)
  starting transfers between devices  16.2 us (5%)
  between operations  13.4 us (4%)
    reduce_scatter x1, waiting for transfers between devices, body(): lax.psum_scatter(jnp.dot(hidden, w_down, preferred_element_type=jnp.float...  68.9 us
    all_gather x1, waiting for transfers between devices, body(): shard_rows = lax.all_gather(normed, 'tile', axis=0, tiled=True)  64.7 us
    all_gather x1, waiting for transfers between devices, body(): lax.all_gather(select(keys_values, 2), ('tile', 'seq'), axis=0, tiled=True)  52.7 us
    dot_general x1, matrix products, body(): jnp.dot(hidden, w_down, preferred_element_type=jnp.float32)  14.6 us
    all_to_all x1, waiting for transfers between devices, body(): lax.all_to_all(meta_table.reshape(devices, capacity, 3), ('tile', 'seq'),...  9.2 us
    all_gather x1, waiting for transfers between devices, body(): segment_kv = lax.all_gather(keys_values, 'seq', axis=0, tiled=True)  8.69 us
    all_to_all x1, starting transfers between devices, body(): lax.all_to_all(meta_table.reshape(devices, capacity, 3), ('tile', 'seq'),...  8.32 us
    all_to_all x1, starting transfers between devices, body(): lax.all_to_all(payload.reshape(devices, capacity, hidden_width), ('tile',...  7.79 us
  transfers between devices with their start and end apart: 6, of which 6 were waited for; matrix products, arithmetic and copies ran while one was open for 13% of the time, Pallas kernels for 0%

commit v1 on v0

--- a/solution.py
+++ b/solution.py
@@ -140,7 +140,15 @@
         )
         return sampled_rows.reshape(resident_rows // SEGMENT_SPACING, stacked_rows * hidden_width)
 
-    far_kv = lax.all_gather(select(keys_values, 2), ("tile", "seq"), axis=0, tiled=True)
+    far_kv = jnp.concatenate(
+        lax.all_to_all(
+            jnp.stack([select(keys_values, 2)] * lax.axis_size(("tile", "seq"))),
+            ("tile", "seq"),
+            0,
+            0,
+        ),
+        axis=0,
+    )
     far_out, far_lse = attend(
         select(queries, 1).reshape(-1, HEAD_COUNT, HEAD_WIDTH),
         far_kv[:, :hidden_width].reshape(-1, HEAD_COUNT, HEAD_WIDTH),

time: 358 us -> 320 us (0.89)
  local copies, waits for them, and re-layouts: 56.9 us -> 38.6 us
  waiting for transfers between devices: 210 us -> 195 us
  matrix products: 36.7 us -> 29.5 us
  starting transfers between devices: 16.2 us -> 20.7 us
    all_gather x1 -> x0, waiting for transfers between devices: 52.7 us -> none  [body(): lax.all_gather(select(keys_values, 2), ('tile', 'seq'), axis=0, tiled=True)]
    all_to_all x0 -> x1, waiting for transfers between devices: none -> 46.8 us  [body(): lax.all_to_all(jnp.stack([select(keys_values, 2)] * lax.axis_size(('tile'...]
    all_gather x1, waiting for transfers between devices: 8.69 us -> 0.01 us  [body(): segment_kv = lax.all_gather(keys_values, 'seq', axis=0, tiled=True)]
    dot_general x2, matrix products: 6.91 us -> 1.98 us  [attend(): jnp.einsum('hqk,khd->qhd', weights.astype(jnp.bfloat16), values, preferre...]
    all_to_all x0 -> x1, starting transfers between devices: none -> 4.55 us  [body(): lax.all_to_all(jnp.stack([select(keys_values, 2)] * lax.axis_size(('tile'...]
    unnamed x29 -> x37, local copies, waits for them, and re-layouts: 6.38 us -> 2.53 us
  transfers between devices with their start and end apart: 6 -> 6, of which waited for: 6 -> 5; matrix products, arithmetic and copies ran while one was open for 13% -> 11% of each run, Pallas kernels for 0% -> 0%
where the time goes in v1:
time: 320 us; the launch traced here: 319 us
  waiting for transfers between devices  195 us (61%)
  local copies, waits for them, and re-layouts  38.6 us (12%)
  matrix products  29.5 us (9%)
  other arithmetic  21 us (7%)
  starting transfers between devices  20.7 us (6%)
  between operations  13.4 us (4%)
    reduce_scatter x1, waiting for transfers between devices, body(): lax.psum_scatter(jnp.dot(hidden, w_down, preferred_element_type=jnp.float...  68.9 us
    all_gather x1, waiting for transfers between devices, body(): shard_rows = lax.all_gather(normed, 'tile', axis=0, tiled=True)  64.7 us
    all_to_all x1, waiting for transfers between devices, body(): lax.all_to_all(jnp.stack([select(keys_values, 2)] * lax.axis_size(('tile'...  46.8 us
    dot_general x1, matrix products, body(): jnp.dot(hidden, w_down, preferred_element_type=jnp.float32)  14.6 us
    all_to_all x1, waiting for transfers between devices, body(): lax.all_to_all(meta_table.reshape(devices, capacity, 3), ('tile', 'seq'),...  9.2 us
    all_to_all x1, starting transfers between devices, body(): lax.all_to_all(meta_table.reshape(devices, capacity, 3), ('tile', 'seq'),...  8.32 us
    all_to_all x1, starting transfers between devices, body(): lax.all_to_all(payload.reshape(devices, capacity, hidden_width), ('tile',...  7.79 us
  transfers between devices with their start and end apart: 6, of which 5 were waited for; matrix products, arithmetic and copies ran while one was open for 11% of the time, Pallas kernels for 0%

profile of v1, /device:TPU:1, one launch (start us, length us, event | category | flops | bytes accessed | tf_op | source)
XLA Modules:
  0.0 318.6 jit_solution(17096413224237292461)
XLA Ops:
  9.1 2.0 fusion.33
  11.2 64.7 %all-gather.3.cloned.1.call-done = bf16[2048,1536]{1,0:T(8,128)(2,1)} async-done(((bf16[128,1536]{1,0:T(8,128)(2,1)}), bf16[2048,1536]{1,0:T(8,128)(2,1)}) %all-gather.3.cloned.1.call-update) | async-done | bytes 6291472 | tf_op jit(solution)/shard_map/all_gather | solution.py:64
  75.9 6.1 %fusion.70 = f32[2048,256]{1,0:T(8,128)} fusion(bf16[2048,1536]{1,0:T(8,128)(2,1)} %all-gather.3.cloned.1.call-done, bf16[1536,256]{1,0:T(8,128)(2,1)} %param.16), kind=kOutput, calls=%fused_computation.112 | convolution fusion | flops 1610612736 | bytes 9175040 | tf_op jit(solution)/shard_map/dot_general | solution.py:65
  82.0 14.6 %fusion.7 = f32[2048,1536]{1,0:T(8,128)} fusion(bf16[256,1536]{1,0:T(8,128)(2,1)} %param.18, bf16[2048,1536]{1,0:T(8,128)(2,1)} %all-gather.3.cloned.1.call-done, bf16[1536,256]{1,0:T(8,128)(2,1)} %param.17, f32[2048,256]{1,0:T(8,128)} %fusion.70), kind=kOutput, calls=%fused_computation.14 | convolution fusion | flops 3224371200 | bytes 22544384 | tf_op jit(solution)/shard_map/dot_general | solution.py:69
  102.0 1.8 scatter_custom_fusion
  103.8 8.3 %all-to-all-start = ((s32[128,2,3]{2,1,0:T(2,128)}), s32[128,2,3]{2,1,0:T(2,128)}, u32[]{:S(2)}, u32[]{:S(2)}) async-start(s32[128,2,3]{2,1,0:T(2,128)} %bitcast.78), calls=%async_computation | async-start | bytes 262144 | tf_op jit(solution)/shard_map/all_to_all | solution.py:98
  112.8 9.2 %all-to-all-done = s32[128,2,3]{2,1,0:T(2,128)} async-done(((s32[128,2,3]{2,1,0:T(2,128)}), s32[128,2,3]{2,1,0:T(2,128)}, u32[]{:S(2)}, u32[]{:S(2)}) %all-to-all-start) | async-done | bytes 3104 | tf_op jit(solution)/shard_map/all_to_all | solution.py:98
  122.0 1.5 copy.82
  123.5 68.9 %reduce-scatter.2.cloned.1.call-done = f32[128,1536]{1,0:T(8,128)} async-done(((f32[2048,1536]{1,0:T(8,128)}), f32[128,1536]{1,0:T(8,128)}) %reduce-scatter.2.cloned.1.call-update) | async-done | bytes 786448 | tf_op jit(solution)/shard_map/reduce_scatter | solution.py:68
  192.4 1.5 fusion.39
  193.9 1.5 multiply_reduce_fusion.1
  195.4 2.9 convolution_convert_fusion.1
  198.3 2.3 scatter_custom_fusion.1
  200.6 1.9 reshape.196
  202.5 7.8 %all-to-all-start.1 = ((bf16[128,2,768]{2,1,0:T(2,128)(2,1)}), bf16[128,2,768]{2,1,0:T(2,128)(2,1)}, u32[]{:S(2)}, u32[]{:S(2)}) async-start(bf16[128,2,768]{2,1,0:T(2,128)(2,1)} %reshape.196), calls=%async_computation.2 | async-start | bytes 786432 | tf_op jit(solution)/shard_map/all_to_all | solution.py:91
  211.0 2.2 scatter_custom_fusion.3
  214.3 2.5 multiply_sine_fusion.1
  216.7 5.6 %all-to-all-done.1 = bf16[128,2,768]{2,1,0:T(2,128)(2,1)} async-done(((bf16[128,2,768]{2,1,0:T(2,128)(2,1)}), bf16[128,2,768]{2,1,0:T(2,128)(2,1)}, u32[]{:S(2)}, u32[]{:S(2)}) %all-to-all-start.1) | async-done | bytes 393248 | tf_op jit(solution)/shard_map/all_to_all | solution.py:91
  222.3 1.9 reshape.226
  224.2 2.7 scatter_custom_fusion.2
  226.9 1.4 fusion.66
  230.9 1.8 reshape.201
  233.2 1.9 stack.11
  235.1 4.6 %all-to-all-start.2 = ((bf16[128,8,1536]{2,1,0:T(8,128)(2,1)}), bf16[128,8,1536]{2,1,0:T(8,128)(2,1)S(1)}, u32[]{:S(2)}, u32[]{:S(2)}) async-start(bf16[128,8,1536]{2,1,0:T(8,128)(2,1)} %stack.11), calls=%async_computation.3 | async-start | bytes 6291456 | tf_op jit(solution)/shard_map/all_to_all | solution.py:144
  243.4 1.9 select_reduce_fusion.1
  245.3 46.8 %all-to-all-done.2 = bf16[128,8,1536]{2,1,0:T(8,128)(2,1)S(1)} async-done(((bf16[128,8,1536]{2,1,0:T(8,128)(2,1)}), bf16[128,8,1536]{2,1,0:T(8,128)(2,1)S(1)}, u32[]{:S(2)}, u32[]{:S(2)}) %all-to-all-start.2) | async-done | bytes 3145760 | tf_op jit(solution)/shard_map/all_to_all | solution.py:144
  292.0 1.9 fusion.67
  293.9 1.8 copy.72
  300.4 3.2 %fusion.68 = (bf16[1024,768]{1,0:T(8,128)(2,1)}, bf16[1024,768]{1,0:T(8,128)(2,1)S(1)}) fusion(bf16[1024,1536]{1,0:T(8,128)(2,1)} %all-gather.5.cloned.1.call-done), kind=kLoop, calls=%fused_computation.110 | loop fusion | bytes 6291456 | tf_op jit(solution)/shard_map/slice | solution.py:126
  303.6 1.7 copy.71
  305.3 1.7 copy.74
  309.6 1.4 fusion.26
  (85 shorter events, 25.3 us)
Async XLA Ops:
  6.5 222.0 %copy-start = (bf16[768,2304]{1,0:T(8,128)(2,1)S(1)}, bf16[768,2304]{1,0:T(8,128)(2,1)}, u32[]{:S(2)}) copy-start(bf16[768,2304]{1,0:T(8,128)(2,1)} %param.25) | copy-start | bytes 10616836
  6.5 69.4 %all-gather.3.cloned.1.call-start = ((), (), s32[]{:S(2)}) async-start(), calls=%async_computation.4 | async-start | bytes 6684672 | tf_op jit(solution)/shard_map/all_gather | solution.py:64
  11.1 181.2 %reduce-scatter.2.cloned.1.call-start = ((), (), s32[]{:S(2)}) async-start(), calls=%async_computation.5 | async-start | bytes 13369344 | tf_op jit(solution)/shard_map/reduce_scatter | solution.py:68
  96.6 95.8 %copy-start.12 = (f32[1536]{0:T(1024)S(1)}, f32[1536]{0:T(1024)}, u32[]{:S(2)}) copy-start(f32[1536]{0:T(1024)} %param.19) | copy-start | bytes 18436
  96.6 98.8 %copy-start.14 = (f32[1536]{0:T(1024)S(1)}, f32[1536]{0:T(1024)}, u32[]{:S(2)}) copy-start(f32[1536]{0:T(1024)} %param.20) | copy-start | bytes 18436
  103.8 18.1 %all-to-all-start = ((s32[128,2,3]{2,1,0:T(2,128)}), s32[128,2,3]{2,1,0:T(2,128)}, u32[]{:S(2)}, u32[]{:S(2)}) async-start(s32[128,2,3]{2,1,0:T(2,128)} %bitcast.78), calls=%async_computation | async-start | bytes 262144 | tf_op jit(solution)/shard_map/all_to_all | solution.py:98
  192.4 3.0 copy-start.2
  192.4 3.0 copy-start.3
  200.6 28.0 %copy-start.16 = (f32[768]{0:T(1024)S(1)}, f32[768]{0:T(1024)}, u32[]{:S(2)}) copy-start(f32[768]{0:T(1024)} %param.24) | copy-start | bytes 9220
  202.5 19.8 %all-to-all-start.1 = ((bf16[128,2,768]{2,1,0:T(2,128)(2,1)}), bf16[128,2,768]{2,1,0:T(2,128)(2,1)}, u32[]{:S(2)}, u32[]{:S(2)}) async-start(bf16[128,2,768]{2,1,0:T(2,128)(2,1)} %reshape.196), calls=%async_computation.2 | async-start | bytes 786432 | tf_op jit(solution)/shard_map/all_to_all | solution.py:91
  210.3 90.1 %all-gather.5.cloned.1.call-start = ((), (), s32[]{:S(2)}) async-start(), calls=%async_computation.6 | async-start | bytes 3538944 | tf_op jit(solution)/shard_map/all_gather | solution.py:123
  228.3 0.9 copy-start.5
  228.5 2.3 copy-start.17
  229.2 0.8 copy-start.7
  235.1 56.9 %all-to-all-start.2 = ((bf16[128,8,1536]{2,1,0:T(8,128)(2,1)}), bf16[128,8,1536]{2,1,0:T(8,128)(2,1)S(1)}, u32[]{:S(2)}, u32[]{:S(2)}) async-start(bf16[128,8,1536]{2,1,0:T(8,128)(2,1)} %stack.11), calls=%async_computation.3 | async-start | bytes 6291456 | tf_op jit(solution)/shard_map/all_to_all | solution.py:144
  293.9 4.0 %copy-start.4 = (bf16[1024,768]{1,0:T(8,128)(2,1)S(1)}, bf16[1024,768]{1,0:T(8,128)(2,1)}, u32[]{:S(2)}) copy-start(bf16[1024,768]{1,0:T(8,128)(2,1)} %get-tuple-element.12) | copy-start | bytes 4718596
  305.3 1.7 copy-start.10
  308.1 1.3 copy-start.13
  308.1 1.3 copy-start.15
  308.1 1.4 copy-start.8
  308.1 1.5 copy-start.11
  309.6 1.4 copy-start.6
  309.6 1.4 copy-start.9
  309.6 2.5 copy-start.1
Sparse Core Ops, SparseCore 0:
  11.3 64.6 all-gather.2
  96.7 95.5 reduce-scatter.1
  231.0 45.6 all-gather.4
